TPU v7x, 32 devices: a whole 2x2x4 slice. The times are simulated.
32 devices in a mesh: crops: 8 (over z, x), rows: 4 (over y, core).
Axes of the slice: x: 2, y: 2, z: 4, core: 2. Of those that a mesh axis runs over, the one named last changes fastest.
Arguments:
- features: bfloat16 [640, 8, 8, 2048], P('crops', 'rows'), may hold values from -6 to 6
- pixel_mask: int32 [640, 8, 8], P('crops', 'rows'), may hold values from 0 to 1, as said below
- partners: int32 [640], P('crops'), may hold values from 0 to 639, as said below
- queued: float32 [3840, 128], P(('crops', 'rows')), as said below
- w_reduce: bfloat16 [2048, 512], P('crops'), may hold values from -0.125 to 0.125
- w_spatial: bfloat16 [4608, 512], P('crops'), may hold values from -0.09375 to 0.09375
- w_expand: bfloat16 [512, 2048], P('crops'), may hold values from -0.25 to 0.25
- w_hidden: bfloat16 [2048, 2048], P('crops'), may hold values from -0.125 to 0.125
- w_embed: bfloat16 [2048, 128], P('crops'), may hold values from -0.125 to 0.125
- prototypes: float32 [128, 3000], replicated, may hold values from -0.75 to 0.75
- gain_one: float32 [512], replicated, may hold values from 0.1 to 1.9
- bias_one: float32 [512], replicated, may hold values from -2.5 to 2.5
- gain_two: float32 [512], replicated, may hold values from 0.1 to 1.9
- bias_two: float32 [512], replicated, may hold values from -2.5 to 2.5
- gain_three: float32 [2048], replicated, may hold values from 0.1 to 1.9
- bias_three: float32 [2048], replicated, may hold values from -2.5 to 2.5
- gain_head: float32 [2048], replicated, may hold values from 0.1 to 1.9
- bias_head: float32 [2048], replicated, may hold values from -2.5 to 2.5
Outputs:
- swav_loss: float32 [], replicated
- grad_features: bfloat16 [640, 8, 8, 2048], P('crops', 'rows')
- grad_w_reduce: float32 [2048, 512], P('crops')
- grad_w_spatial: float32 [4608, 512], P('crops')
- grad_w_expand: float32 [512, 2048], P('crops')
- grad_w_hidden: float32 [2048, 2048], P('crops')
- grad_w_embed: float32 [2048, 128], P('crops')
- grad_prototypes: float32 [128, 3000], replicated
- grad_gain_one: float32 [512], replicated
- grad_bias_one: float32 [512], replicated
- grad_gain_two: float32 [512], replicated
- grad_bias_two: float32 [512], replicated
- grad_gain_three: float32 [2048], replicated
- grad_bias_three: float32 [2048], replicated
- grad_gain_head: float32 [2048], replicated
- grad_bias_head: float32 [2048], replicated
Inputs may be any that keep to these rules, and one draw needn't show every extreme that they name: `pixel_mask`: each crop's valid pixels form one rectangle of 7 x 7 or 6 x 8 pixels inside its map. partners[n] != n, partners[partners[n]] == n, and n and partners[n] lie in the same aligned block of 80 crops. `queued`: every row has a nonzero entry.
All inputs are finite; a program needn't handle non-finite values.
Results may differ from a plain program's by a relative error of at most 0.012.
Values may be sent and summed in bfloat16 or wider, within the bound.
No kernel may reach another device: no remote copies, remote signals or barrier semaphores. Data moves between devices by JAX's collectives and lax.ppermute only.
A program may use at most 192 MiB of HBM per device.

v0:
```python
import jax
import jax.numpy as jnp
from jax import lax
from jax.sharding import PartitionSpec as P

EPS_NORM = 1e-05
EPS_UNIT = 1e-06
SHARPNESS = 0.05
SOFTMAX_TEMPER = 0.1
PRECISE = lax.Precision.HIGHEST


def with_halo(cells, sides, width):
    for axis, dim in sides:
        count = lax.axis_size(axis)
        ends = count - 1
        head = lax.slice_in_dim(cells, 0, width, axis=dim)
        tail = lax.slice_in_dim(cells, cells.shape[dim] - width, cells.shape[dim], axis=dim)
        cells = jnp.concatenate(
            [
                lax.ppermute(tail, axis, [(i, (i + 1) % count) for i in range(ends)]),
                cells,
                lax.ppermute(head, axis, [((i + 1) % count, i) for i in range(ends)]),
            ],
            axis=dim,
        )
    return cells


def moments(value_entries, weights):
    first_sum = jnp.sum(value_entries * weights, axis=0)
    second_sum = jnp.sum(value_entries * value_entries * weights, axis=0)
    total_sum, square_sum, valid_count = lax.psum(
        (first_sum, second_sum, jnp.sum(weights)), ("crops", "rows")
    )
    col_mean = total_sum / valid_count
    spread = lax.rsqrt(square_sum / valid_count - col_mean * col_mean + EPS_NORM)
    return (col_mean, spread, valid_count)


def norm_back(upstream, normed, weights, gain, spread, valid_count):
    grad_gain, grad_bias = lax.psum(
        (jnp.sum(upstream * normed, axis=0), jnp.sum(upstream, axis=0)), ("crops", "rows")
    )
    grad_input = (
        weights * (gain * spread) * (upstream - (grad_bias + normed * grad_gain) / valid_count)
    )
    return (grad_input, grad_gain, grad_bias)


def gelu_back(inputs, upstream):
    return jax.vjp(jax.nn.gelu, inputs)[1](upstream)[0]


def tap_columns(extended, height, breadth):
    padded = jnp.pad(extended, ((0, 0), (0, 0), (1, 1), (0, 0)))
    pieces = [
        padded[:, tap_row : tap_row + height, tap_col : tap_col + breadth, :]
        for tap_row in range(3)
        for tap_col in range(3)
    ]
    return jnp.concatenate(pieces, axis=-1).reshape(-1, 9 * extended.shape[3])


def block_forward(features, pixel_mask, weights, params, kept_stats):
    w_reduce, w_spatial, w_expand = weights
    gain_one, bias_one, gain_two, bias_two, gain_three, bias_three = params
    local_crops, height, breadth, channels = features.shape
    masked = features * pixel_mask.astype(jnp.bfloat16)[..., None]
    flat_in = masked.reshape(-1, channels)
    weight_col = pixel_mask.reshape(-1, 1).astype(jnp.float32)
    pre_one = jnp.dot(flat_in, w_reduce, preferred_element_type=jnp.float32)
    stat_one = moments(pre_one, weight_col) if kept_stats is None else kept_stats[0]
    norm_one = (pre_one - stat_one[0]) * stat_one[1]
    act_one = gain_one * norm_one + bias_one
    hidden_one = (jax.nn.gelu(act_one) * weight_col).astype(jnp.bfloat16)
    grid_one = hidden_one.reshape(local_crops, height, breadth, -1)
    extended = with_halo(grid_one, (("rows", 1),), 1)
    columns = tap_columns(extended, height, breadth)
    pre_two = jnp.dot(columns, w_spatial, preferred_element_type=jnp.float32)
    stat_two = moments(pre_two, weight_col) if kept_stats is None else kept_stats[1]
    norm_two = (pre_two - stat_two[0]) * stat_two[1]
    act_two = gain_two * norm_two + bias_two
    hidden_two = (jax.nn.gelu(act_two) * weight_col).astype(jnp.bfloat16)
    pre_three = jnp.dot(hidden_two, w_expand, preferred_element_type=jnp.float32)
    stat_three = moments(pre_three, weight_col) if kept_stats is None else kept_stats[2]
    norm_three = (pre_three - stat_three[0]) * stat_three[1]
    summed = gain_three * norm_three + bias_three + flat_in.astype(jnp.float32)
    output = jax.nn.gelu(summed) * weight_col
    kept = (
        flat_in,
        weight_col,
        columns,
        norm_one,
        act_one,
        norm_two,
        act_two,
        hidden_two,
        norm_three,
        summed,
        output,
    )
    return (kept, (stat_one, stat_two, stat_three))


def shards(
    features,
    pixel_mask,
    partners,
    queued,
    w_reduce,
    w_spatial,
    w_expand,
    w_hidden,
    w_embed,
    prototypes,
    gain_one,
    bias_one,
    gain_two,
    bias_two,
    gain_three,
    bias_three,
    gain_head,
    bias_head,
):
    full_reduce, full_spatial, full_expand, full_hidden, full_embed = (
        lax.all_gather(w_reduce, "crops", axis=0, tiled=True),
        lax.all_gather(w_spatial, "crops", axis=0, tiled=True),
        lax.all_gather(w_expand, "crops", axis=0, tiled=True),
        lax.all_gather(w_hidden, "crops", axis=0, tiled=True),
        lax.all_gather(w_embed, "crops", axis=0, tiled=True),
    )
    block_weights = (full_reduce, full_spatial, full_expand)
    block_params = (gain_one, bias_one, gain_two, bias_two, gain_three, bias_three)
    local_crops, height, breadth, channels = features.shape
    kept, stats = block_forward(features, pixel_mask, block_weights, block_params, None)
    output = kept[10]
    crop_sums = jnp.sum(output.reshape(local_crops, height * breadth, channels), axis=1)
    crop_valid = jnp.sum(pixel_mask.reshape(local_crops, -1), axis=1).astype(jnp.float32)
    pooled_sum, crop_count = (
        lax.psum_scatter(crop_sums, "rows", scatter_dimension=0, tiled=True),
        lax.psum_scatter(crop_valid, "rows", scatter_dimension=0, tiled=True),
    )
    pooled = pooled_sum / crop_count[:, None]
    head_matrix = full_hidden.astype(jnp.float32)
    embed_matrix = full_embed.astype(jnp.float32)
    pre_head = jnp.dot(pooled, head_matrix, precision=PRECISE)
    head_ones = jnp.ones((pre_head.shape[0], 1), jnp.float32)
    stat_head = moments(pre_head, head_ones)
    norm_head = (pre_head - stat_head[0]) * stat_head[1]
    projector_activation = gain_head * norm_head + bias_head
    hidden_head = jax.nn.gelu(projector_activation)
    embedding = jnp.dot(hidden_head, embed_matrix, precision=PRECISE)
    inverse = lax.rsqrt(jnp.sum(embedding * embedding, axis=1, keepdims=True) + EPS_UNIT)
    unit_embed = embedding * inverse
    centroid_similarity = jnp.dot(unit_embed, prototypes, precision=PRECISE)
    queue_unit = queued * lax.rsqrt(jnp.sum(queued * queued, axis=1, keepdims=True) + EPS_UNIT)
    stored_similarity = jnp.dot(queue_unit, prototypes, precision=PRECISE)
    total_crops = local_crops * lax.axis_size("crops")
    row_total = total_crops + queued.shape[0] * lax.axis_size("crops") * lax.axis_size("rows")
    proto_total = centroid_similarity.shape[1]
    plan_mass = jnp.exp(centroid_similarity / SHARPNESS)
    queue_mass = jnp.exp(stored_similarity / SHARPNESS)
    for iteration in range(3):
        column = lax.psum(
            jnp.sum(plan_mass, axis=0) + jnp.sum(queue_mass, axis=0), ("crops", "rows")
        )
        plan_mass = plan_mass / (proto_total * column)
        queue_mass = queue_mass / (proto_total * column)
        plan_mass = plan_mass / (row_total * jnp.sum(plan_mass, axis=1, keepdims=True))
        queue_mass = queue_mass / (row_total * jnp.sum(queue_mass, axis=1, keepdims=True))
    balanced_cluster_labels = row_total * plan_mass
    everyone = lax.all_gather(balanced_cluster_labels, "rows", axis=0, tiled=True)
    share_rows = balanced_cluster_labels.shape[0]
    partner_rows = (
        lax.dynamic_slice_in_dim(partners, lax.axis_index("rows") * share_rows, share_rows)
        - lax.axis_index("crops") * local_crops
    )
    swapped_cluster_labels = jnp.take(everyone, partner_rows, axis=0)
    log_probability = jax.nn.log_softmax(centroid_similarity / SOFTMAX_TEMPER, axis=1)
    loss_part = -jnp.sum(swapped_cluster_labels * log_probability) / total_crops
    grad_scores = (
        jnp.exp(log_probability) * jnp.sum(swapped_cluster_labels, axis=1, keepdims=True)
        - swapped_cluster_labels
    ) / (SOFTMAX_TEMPER * total_crops)
    grad_proto_part = jnp.dot(unit_embed.T, grad_scores, precision=PRECISE)
    grad_unit = jnp.dot(grad_scores, prototypes.T, precision=PRECISE)
    grad_embedding = inverse * (
        grad_unit - unit_embed * jnp.sum(unit_embed * grad_unit, axis=1, keepdims=True)
    )
    grad_w_embed = jnp.dot(hidden_head.T, grad_embedding, precision=PRECISE)
    grad_hidden_head = jnp.dot(grad_embedding, embed_matrix.T, precision=PRECISE)
    grad_act_head = gelu_back(projector_activation, grad_hidden_head)
    grad_gain_head, grad_bias_head, grad_prototypes, swav_loss = lax.psum(
        (
            jnp.sum(grad_act_head * norm_head, axis=0),
            jnp.sum(grad_act_head, axis=0),
            grad_proto_part,
            loss_part,
        ),
        ("crops", "rows"),
    )
    grad_pre_head = (
        gain_head
        * stat_head[1]
        * (grad_act_head - (grad_bias_head + norm_head * grad_gain_head) / stat_head[2])
    )
    grad_w_hidden = jnp.dot(pooled.T, grad_pre_head, precision=PRECISE)
    grad_pooled = jnp.dot(grad_pre_head, head_matrix.T, precision=PRECISE)
    per_pixel = grad_pooled / crop_count[:, None]
    scale_rows = lax.all_gather(per_pixel, "rows", axis=0, tiled=True)
    kept, stats = block_forward(features, pixel_mask, block_weights, block_params, stats)
    (
        flat_in,
        weight_col,
        columns,
        norm_one,
        act_one,
        norm_two,
        act_two,
        hidden_two,
        norm_three,
        summed,
        output,
    ) = kept
    stat_one, stat_two, stat_three = stats
    grad_output = (
        scale_rows[:, None, :] * weight_col.reshape(local_crops, height * breadth, 1)
    ).reshape(-1, channels)
    grad_summed = gelu_back(summed, grad_output)
    grad_pre_three, grad_gain_three, grad_bias_three = norm_back(
        grad_summed, norm_three, weight_col, gain_three, stat_three[1], stat_three[2]
    )
    grad_pre_three = grad_pre_three.astype(jnp.bfloat16)
    grad_w_expand = jnp.dot(hidden_two.T, grad_pre_three, preferred_element_type=jnp.float32)
    grad_hidden_two = jnp.dot(grad_pre_three, full_expand.T, preferred_element_type=jnp.float32)
    grad_act_two = gelu_back(act_two, grad_hidden_two * weight_col)
    grad_pre_two, grad_gain_two, grad_bias_two = norm_back(
        grad_act_two, norm_two, weight_col, gain_two, stat_two[1], stat_two[2]
    )
    grad_pre_two = grad_pre_two.astype(jnp.bfloat16)
    grad_w_spatial = jnp.dot(columns.T, grad_pre_two, preferred_element_type=jnp.float32)
    narrow = grad_pre_two.shape[1]
    grad_grid = grad_pre_two.reshape(local_crops, height, breadth, narrow)
    grad_extended = with_halo(grad_grid, (("rows", 1),), 1)
    spatial_back = (
        full_spatial.reshape(9, -1, narrow)[::-1].transpose(0, 2, 1).reshape(9 * narrow, -1)
    )
    grad_hidden_one = jnp.dot(
        tap_columns(grad_extended, height, breadth),
        spatial_back,
        preferred_element_type=jnp.float32,
    )
    grad_act_one = gelu_back(act_one, grad_hidden_one * weight_col)
    grad_pre_one, grad_gain_one, grad_bias_one = norm_back(
        grad_act_one, norm_one, weight_col, gain_one, stat_one[1], stat_one[2]
    )
    grad_pre_one = grad_pre_one.astype(jnp.bfloat16)
    grad_w_reduce = jnp.dot(flat_in.T, grad_pre_one, preferred_element_type=jnp.float32)
    grad_features = (
        (
            (jnp.dot(grad_pre_one, full_reduce.T, preferred_element_type=jnp.float32) + grad_summed)
            * weight_col
        )
        .astype(jnp.bfloat16)
        .reshape(features.shape)
    )
    sum_reduce, sum_spatial, sum_expand, sum_hidden, sum_embed = (
        lax.psum_scatter(grad_w_reduce, "crops", scatter_dimension=0, tiled=True),
        lax.psum_scatter(grad_w_spatial, "crops", scatter_dimension=0, tiled=True),
        lax.psum_scatter(grad_w_expand, "crops", scatter_dimension=0, tiled=True),
        lax.psum_scatter(grad_w_hidden, "crops", scatter_dimension=0, tiled=True),
        lax.psum_scatter(grad_w_embed, "crops", scatter_dimension=0, tiled=True),
    )
    out_reduce, out_spatial, out_expand, out_hidden, out_embed = lax.psum(
        (sum_reduce, sum_spatial, sum_expand, sum_hidden, sum_embed), "rows"
    )
    return (
        swav_loss,
        grad_features,
        out_reduce,
        out_spatial,
        out_expand,
        out_hidden,
        out_embed,
        grad_prototypes,
        grad_gain_one,
        grad_bias_one,
        grad_gain_two,
        grad_bias_two,
        grad_gain_three,
        grad_bias_three,
        grad_gain_head,
        grad_bias_head,
    )


def solution(mesh):
    in_specs = (
        P("crops", "rows", None, None),
        P("crops", "rows", None),
        P("crops"),
        P(("crops", "rows"), None),
        P("crops", None),
        P("crops", None),
        P("crops", None),
        P("crops", None),
        P("crops", None),
        P(),
        P(),
        P(),
        P(),
        P(),
        P(),
        P(),
        P(),
        P(),
    )
    out_specs = (
        P(),
        P("crops", "rows", None, None),
        P("crops", None),
        P("crops", None),
        P("crops", None),
        P("crops", None),
        P("crops", None),
        P(),
        P(),
        P(),
        P(),
        P(),
        P(),
        P(),
        P(),
        P(),
    )
    return jax.shard_map(shards, mesh=mesh, in_specs=in_specs, out_specs=out_specs, check_vma=False)
```

profile of v0, /device:TPU:0, one launch (start us, length us, event | category | flops | bytes accessed | tf_op | source)
XLA Modules:
  0.0 1608.6 jit_solution(18232524275703027354)
XLA Ops:
  13.5 5.3 broadcast_multiply_fusion
  18.8 43.4 %all-gather.7.cloned.1.call-done = bf16[2048,512]{1,0:T(8,128)(2,1)} async-done(((bf16[256,512]{1,0:T(8,128)(2,1)}), bf16[2048,512]{1,0:T(8,128)(2,1)}) %all-gather.7.cloned.1.call-update) | async-done | bytes 2097168 | tf_op jit(solution)/shard_map/all_gather | solution.py:127
  62.2 7.7 multiply_reduce_fusion.8
  69.9 40.6 %all-reduce.12 = (f32[512]{0:T(512)S(1)}, f32[]{:T(128)}, f32[512]{0:T(512)S(1)}) all-reduce(f32[512]{0:T(512)S(1)} %get-tuple-element.23, f32[]{:T(128)} %convert_reduce_fusion, f32[512]{0:T(512)S(1)} %get-tuple-element.22), channel_id=1, replica_groups=mesh['crops'=8,'rows'=4] {'crops','rows'}, use_global_device_ids=true, to_apply=%region_5.0 | all-reduce | flops 1025 | bytes 8200 | tf_op jit(solution)/shard_map/psum | solution.py:33
  111.8 3.0 multiply_convert_fusion.5
  117.0 2.8 collective-permute-start
  123.0 9.4 all-reduce.3
  133.2 34.4 %all_gather.25 = bf16[2048,128]{1,0:T(8,128)(2,1)} all-gather(bf16[256,128]{1,0:T(8,128)(2,1)S(1)} %copy-done.27), channel_id=1, replica_groups=mesh['crops'=8,'rows'=4] {'crops'}, dimensions={0}, use_global_device_ids=true | all-gather | bytes 589824 | tf_op jit(solution)/shard_map/all_gather | solution.py:131
  171.4 3.8 select_maximum_fusion.2
  189.2 11.7 multiply_reduce_fusion.6
  200.8 42.9 %all-reduce.11 = (f32[512]{0:T(512)S(1)}, f32[512]{0:T(512)S(1)}) all-reduce(f32[512]{0:T(512)S(1)} %get-tuple-element.21, f32[512]{0:T(512)S(1)} %get-tuple-element.20), channel_id=1, replica_groups=mesh['crops'=8,'rows'=4] {'crops','rows'}, use_global_device_ids=true, to_apply=%region_9.10 | all-reduce | flops 1024 | bytes 8192 | tf_op jit(solution)/shard_map/psum | solution.py:33
  245.0 8.8 multiply_reduce_fusion.1
  253.8 45.8 %all-reduce.10 = (f32[2048]{0:T(1024)S(1)}, f32[2048]{0:T(1024)S(1)}) all-reduce(f32[2048]{0:T(1024)S(1)} %get-tuple-element.17, f32[2048]{0:T(1024)S(1)} %get-tuple-element.16), channel_id=1, replica_groups=mesh['crops'=8,'rows'=4] {'crops','rows'}, use_global_device_ids=true, to_apply=%region_11.12 | all-reduce | flops 4096 | bytes 32768 | tf_op jit(solution)/shard_map/psum | solution.py:33
  301.5 13.3 multiply_multiply_fusion.2
  314.8 7.1 reduce_sum.344
  322.0 13.7 fusion
  340.2 5.9 fusion.86
  346.2 45.6 %all-reduce.9 = (f32[2048]{0:T(1024)S(1)}, f32[]{:T(128)}, f32[2048]{0:T(1024)S(1)}) all-reduce(f32[2048]{0:T(1024)S(1)} %get-tuple-element.37, f32[]{:T(128)} %constant.39.clone.1, f32[2048]{0:T(1024)S(1)} %get-tuple-element.36), channel_id=1, replica_groups=mesh['crops'=8,'rows'=4] {'crops','rows'}, use_global_device_ids=true, to_apply=%region_22.23 | all-reduce | flops 4097 | bytes 32776 | tf_op jit(solution)/shard_map/psum | solution.py:33
  397.5 40.5 %psum.212 = f32[3000]{0:T(1024)} all-reduce(f32[3000]{0:T(1024)} %add.273), channel_id=1, replica_groups=mesh['crops'=8,'rows'=4] {'crops','rows'}, use_global_device_ids=true, to_apply=%region_27.28 | all-reduce | flops 3000 | bytes 24000 | tf_op jit(solution)/shard_map/psum | solution.py:165
  441.3 40.8 %psum.213 = f32[3000]{0:T(1024)} all-reduce(f32[3000]{0:T(1024)} %add.274), channel_id=1, replica_groups=mesh['crops'=8,'rows'=4] {'crops','rows'}, use_global_device_ids=true, to_apply=%region_32.33 | all-reduce | flops 3000 | bytes 24000 | tf_op jit(solution)/shard_map/psum | solution.py:165
  487.2 40.9 %psum.214 = f32[3000]{0:T(1024)S(1)} all-reduce(f32[3000]{0:T(1024)S(1)} %add.275), channel_id=1, replica_groups=mesh['crops'=8,'rows'=4] {'crops','rows'}, use_global_device_ids=true, to_apply=%region_37.38 | all-reduce | flops 3000 | bytes 24000 | tf_op jit(solution)/shard_map/psum | solution.py:165
  529.9 12.0 all-gather
  546.9 2.8 fusion.56
  549.8 37.9 %all-reduce.8 = (f32[2048]{0:T(1024)S(1)}, f32[2048]{0:T(1024)S(1)}) all-reduce(f32[2048]{0:T(1024)S(1)} %get-tuple-element.35, f32[2048]{0:T(1024)S(1)} %get-tuple-element.34), channel_id=1, replica_groups=mesh['crops'=8,'rows'=4] {'crops','rows'}, use_global_device_ids=true, to_apply=%region_48.49 | all-reduce | flops 4096 | bytes 32768 | tf_op jit(solution)/shard_map/psum | solution.py:194
  587.7 9.6 fusion.27
  597.3 9.4 all-gather.1
  607.4 15.0 fusion.82
  622.4 40.0 %all-reduce.7 = (f32[2048]{0:T(1024)S(1)}, f32[2048]{0:T(1024)S(1)}) all-reduce(f32[2048]{0:T(1024)S(1)} %get-tuple-element.19, f32[2048]{0:T(1024)S(1)} %get-tuple-element.18), channel_id=1, replica_groups=mesh['crops'=8,'rows'=4] {'crops','rows'}, use_global_device_ids=true, to_apply=%region_52.53 | all-reduce | flops 4096 | bytes 32768 | tf_op jit(solution)/shard_map/psum | solution.py:42
  662.4 10.0 multiply_convert_fusion.1
  672.5 6.3 fusion.84
  678.7 39.6 %all-reduce.6 = (f32[512]{0:T(512)S(1)}, f32[512]{0:T(512)S(1)}) all-reduce(f32[512]{0:T(512)S(1)} %get-tuple-element.27, f32[512]{0:T(512)S(1)} %get-tuple-element.26), channel_id=1, replica_groups=mesh['crops'=8,'rows'=4] {'crops','rows'}, use_global_device_ids=true, to_apply=%region_56.57 | all-reduce | flops 1024 | bytes 8192 | tf_op jit(solution)/shard_map/psum | solution.py:42
  718.4 8.9 fusion.80
  728.0 4.2 multiply_convert_fusion.3
  738.7 6.7 copy.42
  747.3 3.6 select_maximum_fusion
  756.5 10.2 fusion.83
  766.7 44.4 %all-reduce.5 = (f32[]{:T(128)}, f32[512]{0:T(512)S(1)}, f32[512]{0:T(512)S(1)}) all-reduce(f32[]{:T(128)S(6)} %div.220, f32[512]{0:T(512)S(1)} %get-tuple-element.25, f32[512]{0:T(512)S(1)} %get-tuple-element.24), channel_id=1, replica_groups=mesh['crops'=8,'rows'=4] {'crops','rows'}, use_global_device_ids=true, to_apply=%region_42.43 | all-reduce | flops 1025 | bytes 8200 | tf_op jit(solution)/shard_map/psum | solution.py:194
  811.1 4.0 multiply_convert_fusion.2
  816.2 7.1 fusion.97
  823.4 13.3 fusion.98
  837.7 16.8 %fusion.58 = f32[2048,2048]{1,0:T(8,128)} fusion(f32[36,2048]{1,0:T(8,128)S(1)} %copy-done.9, u32[]{:S(6)} %subtract, f32[20]{0:T(128)S(1)} %copy-done.43, f32[20,2048]{1,0:T(8,128)S(1)} %get-tuple-element.112, f32[20,2048]{1,0:T(8,128)S(1)} %get-tuple-element.104, f32[]{:T(128)} %get-tuple-element.48, f32[2048]{0:T(1024)S(1)} %get-tuple-element.129, ...), kind=kOutput, calls=%fused_computation.144 | convolution fusion | flops 1006960640 | bytes 17408520 | tf_op jit(solution)/shard_map/dot_general | solution.py:208
  855.2 3.8 fusion.60
  859.2 52.8 %reduce-scatter.8.cloned.1.call-done = f32[256,512]{1,0:T(8,128)} async-done(((f32[2048,512]{1,0:T(8,128)}), f32[256,512]{1,0:T(8,128)}) %reduce-scatter.8.cloned.1.call-update) | async-done | bytes 524304 | tf_op jit(solution)/shard_map/reduce_scatter | solution.py:269
  912.0 167.3 %reduce-scatter.10.cloned.1.call-done = f32[576,512]{1,0:T(8,128)} async-done(((f32[4608,512]{1,0:T(8,128)}), f32[576,512]{1,0:T(8,128)}) %reduce-scatter.10.cloned.1.call-update) | async-done | bytes 1179664 | tf_op jit(solution)/shard_map/reduce_scatter | solution.py:270
  1079.2 285.3 %reduce-scatter.14.cloned.1.call-done = f32[256,2048]{1,0:T(8,128)} async-done(((f32[2048,2048]{1,0:T(8,128)}), f32[256,2048]{1,0:T(8,128)}) %reduce-scatter.14.cloned.1.call-update) | async-done | bytes 2097168 | tf_op jit(solution)/shard_map/reduce_scatter | solution.py:272
  1364.5 7.8 multiply_convert_fusion
  1372.3 128.8 %all-reduce.17.cloned.1.call-done = f32[128,3000]{0,1:T(8,128)} async-done(((f32[128,3000]{0,1:T(8,128)}), f32[128,3000]{0,1:T(8,128)}) %all-reduce.17.cloned.1.call-update) | async-done | bytes 1536016 | tf_op jit(solution)/shard_map/psum | solution.py:194
  1501.1 92.4 %all-reduce.19.cloned.1.call-done = (f32[256,512]{1,0:T(8,128)}, f32[576,512]{1,0:T(8,128)}, f32[64,2048]{1,0:T(8,128)}, f32[256,2048]{1,0:T(8,128)}, f32[256,128]{1,0:T(8,128)}) async-done(((f32[256,512]{1,0:T(8,128)}, f32[576,512]{1,0:T(8,128)}, f32[64,2048]{1,0:T(8,128)}, f32[256,2048]{1,0:T(8,128)}, f32[256,128]{1,0:T(8,128)}), (f32[256,512]{1,0:T(8,128)}, f32[576,512]{1,0:T(8,128)}, ...) | async-done | bytes 4456464 | tf_op jit(solution)/shard_map/psum | solution.py:275
  (292 shorter events, 84.0 us)
Async XLA Ops:
  7.2 160.4 %copy-start = (f32[128,3000]{0,1:T(8,128)S(1)}, f32[128,3000]{0,1:T(8,128)}, u32[]{:S(2)}) copy-start(f32[128,3000]{0,1:T(8,128)} %param.27) | copy-start | bytes 4608004
  7.2 55.0 %all-gather.7.cloned.1.call-start = ((), (), s32[]{:S(2)}) async-start(), calls=%async_computation.5 | async-start | bytes 2359296 | tf_op jit(solution)/shard_map/all_gather | solution.py:127
  7.9 181.2 %all-gather.9.cloned.1.call-start = ((), (), s32[]{:S(2)}) async-start(), calls=%async_computation.6 | async-start | bytes 5308416 | tf_op jit(solution)/shard_map/all_gather | solution.py:128
  8.7 236.3 %all-gather.11.cloned.1.call-start = ((), (), s32[]{:S(2)}) async-start(), calls=%async_computation.7 | async-start | bytes 2359296 | tf_op jit(solution)/shard_map/all_gather | solution.py:129
  9.4 330.8 %all-gather.13.cloned.1.call-start = ((), (), s32[]{:S(2)}) async-start(), calls=%async_computation.8 | async-start | bytes 9437184 | tf_op jit(solution)/shard_map/all_gather | solution.py:130
  10.0 849.1 %reduce-scatter.16.cloned.1.call-start = ((), (), s32[]{:S(2)}) async-start(), calls=%async_computation.13 | async-start | bytes 1179648 | tf_op jit(solution)/shard_map/reduce_scatter | solution.py:273
  62.2 48.4 %copy-start.39 = (f32[512]{0:T(512)S(1)}, f32[512]{0:T(512)}, u32[]{:S(2)}) copy-start(f32[512]{0:T(512)} %param.28) | copy-start | bytes 6148
  62.2 49.6 %copy-start.59 = (f32[512]{0:T(512)S(1)}, f32[512]{0:T(512)}, u32[]{:S(2)}) copy-start(f32[512]{0:T(512)} %param.29) | copy-start | bytes 6148
  111.8 70.2 %copy-start.29 = (f32[512]{0:T(512)}, f32[512]{0:T(512)S(1)}, u32[]{:S(2)}) copy-start(f32[512]{0:T(512)S(1)} %get-tuple-element.63) | copy-start | bytes 6148
  111.8 70.2 %copy-start.31 = (f32[512]{0:T(512)}, f32[512]{0:T(512)S(1)}, u32[]{:S(2)}) copy-start(f32[512]{0:T(512)S(1)} %get-tuple-element.98) | copy-start | bytes 6148
  111.8 20.7 %copy-start.78 = (s32[80]{0:T(128)S(1)}, s32[80]{0:T(128)}, u32[]{:S(2)}) copy-start(s32[80]{0:T(128)} %param.20) | copy-start | bytes 964
  111.8 21.4 %copy-start.27 = (bf16[256,128]{1,0:T(8,128)(2,1)S(1)}, bf16[256,128]{1,0:T(8,128)(2,1)}, u32[]{:S(2)}) copy-start(bf16[256,128]{1,0:T(8,128)(2,1)} %param.26) | copy-start | bytes 196612
  114.8 52.8 %copy-start.15 = (f32[120,128]{1,0:T(8,128)S(1)}, f32[120,128]{1,0:T(8,128)}, u32[]{:S(2)}) copy-start(f32[120,128]{1,0:T(8,128)} %param.21) | copy-start | bytes 184324
  117.0 52.8 %collective-permute-start = (bf16[80,1,8,512]{3,2,1,0:T(8,128)(2,1)}, bf16[80,1,8,512]{3,2,1,0:T(8,128)(2,1)}, u32[]{:S(2)}, u32[]{:S(2)}) collective-permute-start(bf16[80,1,8,512]{3,2,1,0:T(8,128)(2,1)} %get-tuple-element.89), channel_id=1, source_target_pairs={{0,1},{1,2},{2,3},{4,5},{5,6},{6,7},{8,9},{9,10},{10,11},{12,13},{... | collective-permute-start | bytes 1966088 | tf_op jit(solution)/shard_map/ppermute | solution.py:21
  119.8 50.1 %collective-permute-start.1 = (bf16[80,1,8,512]{3,2,1,0:T(8,128)(2,1)}, bf16[80,1,8,512]{3,2,1,0:T(8,128)(2,1)}, u32[]{:S(2)}, u32[]{:S(2)}) collective-permute-start(bf16[80,1,8,512]{3,2,1,0:T(8,128)(2,1)} %get-tuple-element.90), channel_id=1, source_target_pairs={{1,0},{2,1},{3,2},{5,4},{6,5},{7,6},{9,8},{10,9},{11,10},{13,12},{... | collective-permute-start | bytes 1966088 | tf_op jit(solution)/shard_map/ppermute | solution.py:23
  132.4 37.5 %copy-start.5 = (bf16[1280,512]{1,0:T(8,128)(2,1)S(1)}, bf16[1280,512]{1,0:T(8,128)(2,1)}, u32[]{:S(2)}) copy-start(bf16[1280,512]{1,0:T(8,128)(2,1)} %copy-done.4) | copy-start | bytes 3932164
  132.5 207.8 %copy-start.41 = (f32[20]{0:T(128)}, f32[20]{0:T(128)S(1)}, u32[]{:S(2)}) copy-start(f32[20]{0:T(128)S(1)} %dynamic-slice.3) | copy-start | bytes 244
  189.2 54.5 %copy-start.75 = (f32[512]{0:T(512)S(1)}, f32[512]{0:T(512)}, u32[]{:S(2)}) copy-start(f32[512]{0:T(512)} %param.30) | copy-start | bytes 6148
  189.2 55.8 %copy-start.80 = (f32[512]{0:T(512)S(1)}, f32[512]{0:T(512)}, u32[]{:S(2)}) copy-start(f32[512]{0:T(512)} %param.31) | copy-start | bytes 6148
  244.9 54.6 %copy-start.23 = (f32[2048]{0:T(1024)S(1)}, f32[2048]{0:T(1024)}, u32[]{:S(2)}) copy-start(f32[2048]{0:T(1024)} %param.32) | copy-start | bytes 24580
  244.9 56.5 %copy-start.33 = (f32[2048]{0:T(1024)S(1)}, f32[2048]{0:T(1024)}, u32[]{:S(2)}) copy-start(f32[2048]{0:T(1024)} %param.33) | copy-start | bytes 24580
  301.5 13.4 copy-start.16
  335.7 2.3 collective-permute-start.4
  340.2 51.5 %copy-start.35 = (f32[2048]{0:T(1024)S(1)}, f32[2048]{0:T(1024)}, u32[]{:S(2)}) copy-start(f32[2048]{0:T(1024)} %param.34) | copy-start | bytes 24580
  340.2 52.8 %copy-start.57 = (f32[2048]{0:T(1024)S(1)}, f32[2048]{0:T(1024)}, u32[]{:S(2)}) copy-start(f32[2048]{0:T(1024)} %param.35) | copy-start | bytes 24580
  394.6 45.1 %copy-start.61 = (f32[20]{0:T(128)}, f32[20]{0:T(128)S(1)}, u32[]{:S(2)}) copy-start(f32[20]{0:T(128)S(1)} %add_rsqrt_fusion.5) | copy-start | bytes 244
  396.2 43.5 %copy-start.46 = (f32[20]{0:T(128)}, f32[20]{0:T(128)S(1)}, u32[]{:S(2)}) copy-start(f32[20]{0:T(128)S(1)} %get-tuple-element.32) | copy-start | bytes 244
  545.1 42.6 %copy-start.25 = (f32[2048]{0:T(1024)S(1)}, f32[2048]{0:T(1024)}, u32[]{:S(2)}) copy-start(f32[2048]{0:T(1024)} %get-tuple-element.91) | copy-start | bytes 24580
  545.1 42.6 %copy-start.42 = (f32[20]{0:T(128)S(1)}, f32[20]{0:T(128)}, u32[]{:S(2)}) copy-start(f32[20]{0:T(128)} %copy-done.41) | copy-start | bytes 244
  587.7 249.1 %copy-start.37 = (f32[2048]{0:T(1024)}, f32[2048]{0:T(1024)S(1)}, u32[]{:S(2)}) copy-start(f32[2048]{0:T(1024)S(1)} %get-tuple-element.129) | copy-start | bytes 24580
  587.7 249.1 %copy-start.38 = (f32[2048]{0:T(1024)}, f32[2048]{0:T(1024)S(1)}, u32[]{:S(2)}) copy-start(f32[2048]{0:T(1024)S(1)} %get-tuple-element.130) | copy-start | bytes 24580
  606.9 55.5 %copy-start.28 = (f32[2048]{0:T(1024)S(1)}, f32[2048]{0:T(1024)}, u32[]{:S(2)}) copy-start(f32[2048]{0:T(1024)} %get-tuple-element.66) | copy-start | bytes 24580
  606.9 252.3 %reduce-scatter.12.cloned.1.call-start = ((), (), s32[]{:S(2)}) async-start(), calls=%async_computation.11 | async-start | bytes 4718592 | tf_op jit(solution)/shard_map/reduce_scatter | solution.py:271
  662.4 10.1 copy-start.7
  662.4 10.1 copy-start.54
  662.4 10.1 copy-start.56
  662.4 10.0 copy-start.76
  662.4 10.0 copy-start.79
  662.4 10.0 copy-start.81
  727.3 184.7 %reduce-scatter.8.cloned.1.call-start = ((), (), s32[]{:S(2)}) async-start(), calls=%async_computation.9 | async-start | bytes 4718592 | tf_op jit(solution)/shard_map/reduce_scatter | solution.py:269
  733.3 12.7 collective-permute-start.2
  734.8 11.2 collective-permute-start.3
  756.5 54.6 %copy-start.51 = (f32[512]{0:T(512)S(1)}, f32[512]{0:T(512)}, u32[]{:S(2)}) copy-start(f32[512]{0:T(512)} %get-tuple-element.62) | copy-start | bytes 6148
  823.3 255.9 %reduce-scatter.10.cloned.1.call-start = ((), (), s32[]{:S(2)}) async-start(), calls=%async_computation.10 | async-start | bytes 10616832 | tf_op jit(solution)/shard_map/reduce_scatter | solution.py:270
  836.7 527.8 %reduce-scatter.14.cloned.1.call-start = ((), (), s32[]{:S(2)}) async-start(), calls=%async_computation.12 | async-start | bytes 18874368 | tf_op jit(solution)/shard_map/reduce_scatter | solution.py:272
  854.6 646.6 %all-reduce.17.cloned.1.call-start = ((), (), s32[]{:S(2)}) async-start(), calls=%async_computation.14 | async-start | bytes 3072000 | tf_op jit(solution)/shard_map/psum | solution.py:194
  859.0 505.5 %copy-start.12 = (bf16[1280,512]{1,0:T(8,128)(2,1)S(1)}, bf16[1280,512]{1,0:T(8,128)(2,1)}, u32[]{:S(2)}) copy-start(bf16[1280,512]{1,0:T(8,128)(2,1)} %copy-done.11) | copy-start | bytes 3932164
  859.1 734.4 %all-reduce.19.cloned.1.call-start = ((), (), s32[]{:S(2)}) async-start(), calls=%async_computation.15 | async-start | bytes 8912896 | tf_op jit(solution)/shard_map/psum | solution.py:275
  (54 other events, 215.2 us)
Sparse Core Ops, SparseCore 0:
  10.2 51.9 all-gather.6
  64.4 80.9 all-gather.8
  147.5 48.5 all-gather.10
  198.1 125.5 all-gather.12
  607.0 63.1 reduce-scatter.15
  727.4 88.6 reduce-scatter.11
  823.4 88.4 reduce-scatter.7
  916.0 163.1 reduce-scatter.9
  1083.5 280.9 reduce-scatter.13
  1370.2 130.8 all-reduce.16
  1503.8 89.6 all-reduce.18
where the time goes:
time: 1620 us; the launch traced here: 1610 us
  waiting for transfers between devices  773 us (48%)
  blocking collectives  538 us (33%)
  matrix products  128 us (8%)
  other arithmetic  95 us (6%)
  local copies, waits for them, and re-layouts  48.3 us (3%)
  between operations  17.2 us (1%)
    reduce_scatter x1, waiting for transfers between devices, shards(): lax.psum_scatter(grad_w_hidden, 'crops', scatter_dimension=0, tiled=True)  285 us
    psum x4, blocking collectives, moments(): lax.psum((first_sum, second_sum, jnp.sum(weights)), ('crops', 'rows'))  175 us
    reduce_scatter x1, waiting for transfers between devices, shards(): lax.psum_scatter(grad_w_spatial, 'crops', scatter_dimension=0, tiled=True)  167 us
    psum x1, waiting for transfers between devices, shards(): lax.psum((jnp.sum(grad_act_head * norm_head, axis=0), jnp.sum(grad_act_he...  129 us
    psum x3, blocking collectives, shards(): lax.psum(jnp.sum(plan_mass, axis=0) + jnp.sum(queue_mass, axis=0), ('crop...  122 us
    psum x1, waiting for transfers between devices, shards(): lax.psum((sum_reduce, sum_spatial, sum_expand, sum_hidden, sum_embed), 'r...  92.4 us
    psum x2, blocking collectives, shards(): lax.psum((jnp.sum(grad_act_head * norm_head, axis=0), jnp.sum(grad_act_he...  82.4 us
    psum x2, blocking collectives, norm_back(): lax.psum((jnp.sum(upstream * normed, axis=0), jnp.sum(upstream, axis=0)),...  79.6 us
  transfers between devices with their start and end apart: 16, of which 7 were waited for; matrix products, arithmetic and copies ran while one was open for 14% of the time, Pallas kernels for 0%

commit v1 on v0

--- a/solution.py
+++ b/solution.py
@@ -162,8 +162,11 @@
     plan_mass = jnp.exp(centroid_similarity / SHARPNESS)
     queue_mass = jnp.exp(stored_similarity / SHARPNESS)
     for iteration in range(3):
-        column = lax.psum(
-            jnp.sum(plan_mass, axis=0) + jnp.sum(queue_mass, axis=0), ("crops", "rows")
+        column = jnp.sum(
+            lax.all_gather(
+                jnp.sum(plan_mass, axis=0) + jnp.sum(queue_mass, axis=0), ("crops", "rows")
+            ),
+            axis=0,
         )
         plan_mass = plan_mass / (proto_total * column)
         queue_mass = queue_mass / (proto_total * column)

time: 1620 us -> 1870 us (1.15)
  waiting for transfers between devices: 773 us -> 1160 us
  blocking collectives: 538 us -> 402 us
    unnamed x12 -> x18, waiting for transfers between devices: 3.06 us -> 383 us
    psum x3 -> x0, blocking collectives: 122 us -> none  [shards(): lax.psum(jnp.sum(plan_mass, axis=0) + jnp.sum(queue_mass, axis=0), ('crop...]
  transfers between devices with their start and end apart: 16 -> 19, of which waited for: 7 -> 11; matrix products, arithmetic and copies ran while one was open for 14% -> 12% of each run, Pallas kernels for 0% -> 0%
where the time goes in v1:
time: 1870 us
  waiting for transfers between devices  1160 us (62%)
  blocking collectives  402 us (21%)
  matrix products  128 us (7%)
  other arithmetic  96.4 us (5%)
  local copies, waits for them, and re-layouts  53 us (3%)
    unnamed x18, waiting for transfers between devices  383 us
    reduce_scatter x1, waiting for transfers between devices, shards(): lax.psum_scatter(grad_w_hidden, 'crops', scatter_dimension=0, tiled=True)  285 us
    reduce_scatter x1, waiting for transfers between devices, shards(): lax.psum_scatter(grad_w_spatial, 'crops', scatter_dimension=0, tiled=True)  167 us
    psum x4, blocking collectives, moments(): lax.psum((first_sum, second_sum, jnp.sum(weights)), ('crops', 'rows'))  164 us
    psum x1, waiting for transfers between devices, shards(): lax.psum((jnp.sum(grad_act_head * norm_head, axis=0), jnp.sum(grad_act_he...  130 us
    psum x1, waiting for transfers between devices, shards(): lax.psum((sum_reduce, sum_spatial, sum_expand, sum_hidden, sum_embed), 'r...  92.4 us
    psum x2, blocking collectives, shards(): lax.psum((jnp.sum(grad_act_head * norm_head, axis=0), jnp.sum(grad_act_he...  83.2 us
    psum x2, blocking collectives, norm_back(): lax.psum((jnp.sum(upstream * normed, axis=0), jnp.sum(upstream, axis=0)),...  78.5 us
  transfers between devices with their start and end apart: 19, of which 11 were waited for; matrix products, arithmetic and copies ran while one was open for 12% of the time, Pallas kernels for 0%

profile of v1, /device:TPU:0, one launch (start us, length us, event | category | flops | bytes accessed | tf_op | source)
XLA Modules:
  0.0 1865.1 jit_solution(13753655326703362011)
XLA Ops:
  12.6 5.3 broadcast_multiply_fusion
  17.8 44.4 %all-gather.10.cloned.1.call-done = bf16[2048,512]{1,0:T(8,128)(2,1)} async-done(((bf16[256,512]{1,0:T(8,128)(2,1)}), bf16[2048,512]{1,0:T(8,128)(2,1)}) %all-gather.10.cloned.1.call-update) | async-done | bytes 2097168 | tf_op jit(solution)/shard_map/all_gather | solution.py:127
  62.2 7.7 multiply_reduce_fusion.8
  69.9 40.6 %all-reduce.15 = (f32[512]{0:T(512)S(1)}, f32[]{:T(128)}, f32[512]{0:T(512)S(1)}) all-reduce(f32[512]{0:T(512)S(1)} %get-tuple-element.23, f32[]{:T(128)} %convert_reduce_fusion, f32[512]{0:T(512)S(1)} %get-tuple-element.22), channel_id=1, replica_groups=mesh['crops'=8,'rows'=4] {'crops','rows'}, use_global_device_ids=true, to_apply=%region_5.0 | all-reduce | flops 1025 | bytes 8200 | tf_op jit(solution)/shard_map/psum | solution.py:33
  111.9 3.0 multiply_convert_fusion.5
  123.2 2.5 select_maximum_fusion.2
  139.7 4.4 all-gather.12.cloned.1.call-done
  144.1 11.6 multiply_reduce_fusion.6
  155.7 43.0 %all-reduce.14 = (f32[512]{0:T(512)S(1)}, f32[512]{0:T(512)S(1)}) all-reduce(f32[512]{0:T(512)S(1)} %get-tuple-element.21, f32[512]{0:T(512)S(1)} %get-tuple-element.20), channel_id=1, replica_groups=mesh['crops'=8,'rows'=4] {'crops','rows'}, use_global_device_ids=true, to_apply=%region_9.10 | all-reduce | flops 1024 | bytes 8192 | tf_op jit(solution)/shard_map/psum | solution.py:33
  200.0 9.1 multiply_reduce_fusion.1
  209.1 42.0 %all-reduce.13 = (f32[2048]{0:T(1024)S(1)}, f32[2048]{0:T(1024)S(1)}) all-reduce(f32[2048]{0:T(1024)S(1)} %get-tuple-element.17, f32[2048]{0:T(1024)S(1)} %get-tuple-element.16), channel_id=1, replica_groups=mesh['crops'=8,'rows'=4] {'crops','rows'}, use_global_device_ids=true, to_apply=%region_11.12 | all-reduce | flops 4096 | bytes 32768 | tf_op jit(solution)/shard_map/psum | solution.py:33
  253.2 13.4 multiply_multiply_fusion.2
  266.6 7.1 reduce_sum.371
  273.7 13.9 fusion
  289.0 35.4 %all_gather.37 = bf16[2048,128]{1,0:T(8,128)(2,1)} all-gather(bf16[256,128]{1,0:T(8,128)(2,1)} %param.26), channel_id=1, replica_groups=mesh['crops'=8,'rows'=4] {'crops'}, dimensions={0}, use_global_device_ids=true | all-gather | bytes 589824 | tf_op jit(solution)/shard_map/all_gather | solution.py:131
  326.3 5.7 all-reduce.6
  334.3 5.9 fusion.86
  340.3 38.7 %all-reduce.12 = (f32[2048]{0:T(1024)S(1)}, f32[]{:T(128)}, f32[2048]{0:T(1024)S(1)}) all-reduce(f32[2048]{0:T(1024)S(1)} %get-tuple-element.37, f32[]{:T(128)} %constant.39.clone.1, f32[2048]{0:T(1024)S(1)} %get-tuple-element.36), channel_id=1, replica_groups=mesh['crops'=8,'rows'=4] {'crops','rows'}, use_global_device_ids=true, to_apply=%region_22.23 | all-reduce | flops 4097 | bytes 32776 | tf_op jit(solution)/shard_map/psum | solution.py:33
  385.6 128.0 %all-reduce.25.cloned.1.call-done = f32[96000]{0:T(1024)} async-done(((f32[96000]{0:T(1024)}), f32[96000]{0:T(1024)}) %all-reduce.25.cloned.1.call-update) | async-done | bytes 384016
  522.4 126.5 %all-reduce.27.cloned.1.call-done = f32[96000]{0:T(1024)} async-done(((f32[96000]{0:T(1024)}), f32[96000]{0:T(1024)}) %all-reduce.27.cloned.1.call-update) | async-done | bytes 384016
  659.6 125.3 %all-reduce.29.cloned.1.call-done = f32[96000]{0:T(1024)} async-done(((f32[96000]{0:T(1024)}), f32[96000]{0:T(1024)}) %all-reduce.29.cloned.1.call-update) | async-done | bytes 384016
  788.0 11.1 all-gather.3
  803.9 2.8 fusion.56
  806.7 39.5 %all-reduce.11 = (f32[2048]{0:T(1024)S(1)}, f32[2048]{0:T(1024)S(1)}) all-reduce(f32[2048]{0:T(1024)S(1)} %get-tuple-element.35, f32[2048]{0:T(1024)S(1)} %get-tuple-element.34), channel_id=1, replica_groups=mesh['crops'=8,'rows'=4] {'crops','rows'}, use_global_device_ids=true, to_apply=%region_48.49 | all-reduce | flops 4096 | bytes 32768 | tf_op jit(solution)/shard_map/psum | solution.py:197
  846.2 9.6 fusion.27
  855.8 9.4 all-gather.4
  865.8 15.0 fusion.82
  880.9 38.5 %all-reduce.10 = (f32[2048]{0:T(1024)S(1)}, f32[2048]{0:T(1024)S(1)}) all-reduce(f32[2048]{0:T(1024)S(1)} %get-tuple-element.19, f32[2048]{0:T(1024)S(1)} %get-tuple-element.18), channel_id=1, replica_groups=mesh['crops'=8,'rows'=4] {'crops','rows'}, use_global_device_ids=true, to_apply=%region_52.53 | all-reduce | flops 4096 | bytes 32768 | tf_op jit(solution)/shard_map/psum | solution.py:42
  919.5 10.0 multiply_convert_fusion.1
  929.6 6.3 fusion.84
  935.9 40.0 %all-reduce.9 = (f32[512]{0:T(512)S(1)}, f32[512]{0:T(512)S(1)}) all-reduce(f32[512]{0:T(512)S(1)} %get-tuple-element.27, f32[512]{0:T(512)S(1)} %get-tuple-element.26), channel_id=1, replica_groups=mesh['crops'=8,'rows'=4] {'crops','rows'}, use_global_device_ids=true, to_apply=%region_56.57 | all-reduce | flops 1024 | bytes 8192 | tf_op jit(solution)/shard_map/psum | solution.py:42
  975.9 8.9 fusion.80
  985.5 4.3 multiply_convert_fusion.3
  996.2 6.7 copy.45
  1004.9 3.6 select_maximum_fusion
  1014.1 10.2 fusion.83
  1024.3 43.7 %all-reduce.8 = (f32[]{:T(128)}, f32[512]{0:T(512)S(1)}, f32[512]{0:T(512)S(1)}) all-reduce(f32[]{:T(128)S(6)} %div.220, f32[512]{0:T(512)S(1)} %get-tuple-element.25, f32[512]{0:T(512)S(1)} %get-tuple-element.24), channel_id=1, replica_groups=mesh['crops'=8,'rows'=4] {'crops','rows'}, use_global_device_ids=true, to_apply=%region_42.43 | all-reduce | flops 1025 | bytes 8200 | tf_op jit(solution)/shard_map/psum | solution.py:197
  1068.1 4.0 multiply_convert_fusion.2
  1073.2 7.1 fusion.97
  1080.4 13.3 fusion.98
  1094.7 16.8 fusion.58
  1112.2 3.8 fusion.60
  1116.1 52.4 %reduce-scatter.8.cloned.1.call-done = f32[256,512]{1,0:T(8,128)} async-done(((f32[2048,512]{1,0:T(8,128)}), f32[256,512]{1,0:T(8,128)}) %reduce-scatter.8.cloned.1.call-update) | async-done | bytes 524304 | tf_op jit(solution)/shard_map/reduce_scatter | solution.py:272
  1168.5 166.8 %reduce-scatter.10.cloned.1.call-done = f32[576,512]{1,0:T(8,128)} async-done(((f32[4608,512]{1,0:T(8,128)}), f32[576,512]{1,0:T(8,128)}) %reduce-scatter.10.cloned.1.call-update) | async-done | bytes 1179664 | tf_op jit(solution)/shard_map/reduce_scatter | solution.py:273
  1335.3 284.6 %reduce-scatter.14.cloned.1.call-done = f32[256,2048]{1,0:T(8,128)} async-done(((f32[2048,2048]{1,0:T(8,128)}), f32[256,2048]{1,0:T(8,128)}) %reduce-scatter.14.cloned.1.call-update) | async-done | bytes 2097168 | tf_op jit(solution)/shard_map/reduce_scatter | solution.py:275
  1619.9 7.8 multiply_convert_fusion
  1627.8 129.8 %all-reduce.23.cloned.1.call-done = f32[128,3000]{0,1:T(8,128)} async-done(((f32[128,3000]{0,1:T(8,128)}), f32[128,3000]{0,1:T(8,128)}) %all-reduce.23.cloned.1.call-update) | async-done | bytes 1536016 | tf_op jit(solution)/shard_map/psum | solution.py:197
  1757.6 92.4 %all-reduce.31.cloned.1.call-done = (f32[256,512]{1,0:T(8,128)}, f32[576,512]{1,0:T(8,128)}, f32[64,2048]{1,0:T(8,128)}, f32[256,2048]{1,0:T(8,128)}, f32[256,128]{1,0:T(8,128)}) async-done(((f32[256,512]{1,0:T(8,128)}, f32[576,512]{1,0:T(8,128)}, f32[64,2048]{1,0:T(8,128)}, f32[256,2048]{1,0:T(8,128)}, f32[256,128]{1,0:T(8,128)}), (f32[256,512]{1,0:T(8,128)}, f32[576,512]{1,0:T(8,128)}, ...) | async-done | bytes 4456464 | tf_op jit(solution)/shard_map/psum | solution.py:278
  (299 shorter events, 95.6 us)
Async XLA Ops:
  7.2 111.8 %copy-start = (f32[128,3000]{0,1:T(8,128)S(1)}, f32[128,3000]{0,1:T(8,128)}, u32[]{:S(2)}) copy-start(f32[128,3000]{0,1:T(8,128)} %param.27) | copy-start | bytes 4608004
  7.2 55.0 %all-gather.10.cloned.1.call-start = ((), (), s32[]{:S(2)}) async-start(), calls=%async_computation.5 | async-start | bytes 2359296 | tf_op jit(solution)/shard_map/all_gather | solution.py:127
  7.9 136.2 %all-gather.12.cloned.1.call-start = ((), (), s32[]{:S(2)}) async-start(), calls=%async_computation.6 | async-start | bytes 5308416 | tf_op jit(solution)/shard_map/all_gather | solution.py:128
  8.7 191.3 %all-gather.14.cloned.1.call-start = ((), (), s32[]{:S(2)}) async-start(), calls=%async_computation.7 | async-start | bytes 2359296 | tf_op jit(solution)/shard_map/all_gather | solution.py:129
  9.4 324.9 %all-gather.16.cloned.1.call-start = ((), (), s32[]{:S(2)}) async-start(), calls=%async_computation.8 | async-start | bytes 9437184 | tf_op jit(solution)/shard_map/all_gather | solution.py:130
  10.0 503.6 %all-reduce.25.cloned.1.call-start = ((), (), s32[]{:S(2)}) async-start(), calls=%async_computation.15 | async-start | bytes 770048
  62.2 48.4 %copy-start.37 = (f32[512]{0:T(512)S(1)}, f32[512]{0:T(512)}, u32[]{:S(2)}) copy-start(f32[512]{0:T(512)} %param.28) | copy-start | bytes 6148
  62.2 49.7 %copy-start.56 = (f32[512]{0:T(512)S(1)}, f32[512]{0:T(512)}, u32[]{:S(2)}) copy-start(f32[512]{0:T(512)} %param.29) | copy-start | bytes 6148
  111.9 20.6 %copy-start.27 = (f32[512]{0:T(512)}, f32[512]{0:T(512)S(1)}, u32[]{:S(2)}) copy-start(f32[512]{0:T(512)S(1)} %get-tuple-element.63) | copy-start | bytes 6148
  111.9 20.6 %copy-start.29 = (f32[512]{0:T(512)}, f32[512]{0:T(512)S(1)}, u32[]{:S(2)}) copy-start(f32[512]{0:T(512)S(1)} %get-tuple-element.98) | copy-start | bytes 6148
  115.0 6.3 collective-permute-start
  117.0 6.0 collective-permute-start.1
  139.7 59.0 %copy-start.72 = (f32[512]{0:T(512)S(1)}, f32[512]{0:T(512)}, u32[]{:S(2)}) copy-start(f32[512]{0:T(512)} %param.30) | copy-start | bytes 6148
  139.7 60.3 %copy-start.76 = (f32[512]{0:T(512)S(1)}, f32[512]{0:T(512)}, u32[]{:S(2)}) copy-start(f32[512]{0:T(512)} %param.31) | copy-start | bytes 6148
  200.0 51.1 %copy-start.22 = (f32[2048]{0:T(1024)S(1)}, f32[2048]{0:T(1024)}, u32[]{:S(2)}) copy-start(f32[2048]{0:T(1024)} %param.32) | copy-start | bytes 24580
  200.0 53.2 %copy-start.31 = (f32[2048]{0:T(1024)S(1)}, f32[2048]{0:T(1024)}, u32[]{:S(2)}) copy-start(f32[2048]{0:T(1024)} %param.33) | copy-start | bytes 24580
  253.2 13.4 copy-start.15
  266.6 57.9 %copy-start.74 = (u32[32]{0:T(128)S(1)}, u32[32]{0:T(128)}, u32[]{:S(2)}) copy-start(u32[32]{0:T(128)} %constant.114) | copy-start | bytes 388
  287.7 44.4 %collective-permute-start.4 = (f32[12,2048]{1,0:T(8,128)S(1)}, f32[12,2048]{1,0:T(8,128)S(1)}, u32[]{:S(2)}, u32[]{:S(2)}) collective-permute-start(f32[12,2048]{1,0:T(8,128)S(1)} %slice.121), channel_id=1, source_target_pairs={{0,1},{1,2},{2,3},{4,5},{5,6},{6,7},{8,9},{9,10},{10,11},{12,13},{... | collective-permute-start | bytes 294920
  334.3 44.6 %copy-start.33 = (f32[2048]{0:T(1024)S(1)}, f32[2048]{0:T(1024)}, u32[]{:S(2)}) copy-start(f32[2048]{0:T(1024)} %param.34) | copy-start | bytes 24580
  334.3 45.9 %copy-start.54 = (f32[2048]{0:T(1024)S(1)}, f32[2048]{0:T(1024)}, u32[]{:S(2)}) copy-start(f32[2048]{0:T(1024)} %param.35) | copy-start | bytes 24580
  380.2 135.4 %copy-start.18 = (f32[2048]{0:T(1024)}, f32[2048]{0:T(1024)S(1)}, u32[]{:S(2)}) copy-start(f32[2048]{0:T(1024)S(1)} %get-tuple-element.92) | copy-start | bytes 24580
  380.2 135.4 %copy-start.20 = (f32[2048]{0:T(1024)}, f32[2048]{0:T(1024)S(1)}, u32[]{:S(2)}) copy-start(f32[2048]{0:T(1024)S(1)} %get-tuple-element.93) | copy-start | bytes 24580
  381.8 136.4 %copy-start.58 = (f32[20]{0:T(128)}, f32[20]{0:T(128)S(1)}, u32[]{:S(2)}) copy-start(f32[20]{0:T(128)S(1)} %add_rsqrt_fusion.5) | copy-start | bytes 244
  383.4 135.6 %copy-start.43 = (f32[20]{0:T(128)}, f32[20]{0:T(128)S(1)}, u32[]{:S(2)}) copy-start(f32[20]{0:T(128)S(1)} %get-tuple-element.32) | copy-start | bytes 244
  385.6 263.4 %all-reduce.27.cloned.1.call-start = ((), (), s32[]{:S(2)}) async-start(), calls=%async_computation.16 | async-start | bytes 770048
  522.2 262.7 %all-reduce.29.cloned.1.call-start = ((), (), s32[]{:S(2)}) async-start(), calls=%async_computation.17 | async-start | bytes 770048
  658.1 458.0 %reduce-scatter.16.cloned.1.call-start = ((), (), s32[]{:S(2)}) async-start(), calls=%async_computation.13 | async-start | bytes 1179648 | tf_op jit(solution)/shard_map/reduce_scatter | solution.py:276
  658.9 143.1 %copy-start.61 = (pred[20]{0:T(512)(128)(4,1)}, pred[20]{0:T(512)(128)(4,1)S(1)}, u32[]{:S(2)}) copy-start(pred[20]{0:T(512)(128)(4,1)S(1)} %get-tuple-element.69) | copy-start | bytes 64
  659.6 142.5 %copy-start.64 = (f32[20]{0:T(128)}, f32[20]{0:T(128)S(1)}, u32[]{:S(2)}) copy-start(f32[20]{0:T(128)S(1)} %log.9) | copy-start | bytes 244
  802.0 44.2 %copy-start.24 = (f32[2048]{0:T(1024)S(1)}, f32[2048]{0:T(1024)}, u32[]{:S(2)}) copy-start(f32[2048]{0:T(1024)} %get-tuple-element.91) | copy-start | bytes 24580
  802.0 44.2 %copy-start.40 = (f32[20]{0:T(128)S(1)}, f32[20]{0:T(128)}, u32[]{:S(2)}) copy-start(f32[20]{0:T(128)} %copy-done.39) | copy-start | bytes 244
  846.2 247.6 %copy-start.35 = (f32[2048]{0:T(1024)}, f32[2048]{0:T(1024)S(1)}, u32[]{:S(2)}) copy-start(f32[2048]{0:T(1024)S(1)} %get-tuple-element.129) | copy-start | bytes 24580
  846.2 247.6 %copy-start.36 = (f32[2048]{0:T(1024)}, f32[2048]{0:T(1024)S(1)}, u32[]{:S(2)}) copy-start(f32[2048]{0:T(1024)S(1)} %get-tuple-element.130) | copy-start | bytes 24580
  865.3 54.1 %copy-start.26 = (f32[2048]{0:T(1024)S(1)}, f32[2048]{0:T(1024)}, u32[]{:S(2)}) copy-start(f32[2048]{0:T(1024)} %get-tuple-element.66) | copy-start | bytes 24580
  865.3 250.8 %reduce-scatter.12.cloned.1.call-start = ((), (), s32[]{:S(2)}) async-start(), calls=%async_computation.11 | async-start | bytes 4718592 | tf_op jit(solution)/shard_map/reduce_scatter | solution.py:274
  919.4 10.1 copy-start.5
  919.4 10.1 copy-start.51
  919.4 10.1 copy-start.53
  984.8 183.7 %reduce-scatter.8.cloned.1.call-start = ((), (), s32[]{:S(2)}) async-start(), calls=%async_computation.9 | async-start | bytes 4718592 | tf_op jit(solution)/shard_map/reduce_scatter | solution.py:272
  990.9 12.7 collective-permute-start.2
  992.4 11.2 collective-permute-start.3
  1014.1 53.9 %copy-start.48 = (f32[512]{0:T(512)S(1)}, f32[512]{0:T(512)}, u32[]{:S(2)}) copy-start(f32[512]{0:T(512)} %get-tuple-element.62) | copy-start | bytes 6148
  1080.3 255.0 %reduce-scatter.10.cloned.1.call-start = ((), (), s32[]{:S(2)}) async-start(), calls=%async_computation.10 | async-start | bytes 10616832 | tf_op jit(solution)/shard_map/reduce_scatter | solution.py:273
  1093.7 526.2 %reduce-scatter.14.cloned.1.call-start = ((), (), s32[]{:S(2)}) async-start(), calls=%async_computation.12 | async-start | bytes 18874368 | tf_op jit(solution)/shard_map/reduce_scatter | solution.py:275
  1111.6 646.0 %all-reduce.23.cloned.1.call-start = ((), (), s32[]{:S(2)}) async-start(), calls=%async_computation.14 | async-start | bytes 3072000 | tf_op jit(solution)/shard_map/psum | solution.py:197
  1116.0 503.9 %copy-start.11 = (bf16[1280,512]{1,0:T(8,128)(2,1)S(1)}, bf16[1280,512]{1,0:T(8,128)(2,1)}, u32[]{:S(2)}) copy-start(bf16[1280,512]{1,0:T(8,128)(2,1)} %copy-done.10) | copy-start | bytes 3932164
  1116.0 733.9 %all-reduce.31.cloned.1.call-start = ((), (), s32[]{:S(2)}) async-start(), calls=%async_computation.18 | async-start | bytes 8912896 | tf_op jit(solution)/shard_map/psum | solution.py:278
  (53 other events, 232.1 us)
Sparse Core Ops, SparseCore 0:
  10.2 51.9 all-gather.9
  64.4 79.6 all-gather.11
  146.2 47.5 all-gather.13
  195.8 129.6 all-gather.15
  385.7 127.8 all-reduce.24
  522.3 126.6 all-reduce.26
  658.2 126.6 all-reduce.28
  865.5 61.6 reduce-scatter.15
  984.9 88.2 reduce-scatter.11
  1080.4 87.9 reduce-scatter.7
  1172.1 163.1 reduce-scatter.9
  1338.9 280.9 reduce-scatter.13
  1626.6 130.8 all-reduce.22
  1760.3 89.6 all-reduce.30
